TPU v7x, 32 devices: a whole 2x2x4 slice. The times are simulated.
32 devices in a mesh: gz: 8 (over z, core), gy: 4 (over y, x).
Axes of the slice: x: 2, y: 2, z: 4, core: 2. Of those that a mesh axis runs over, the one named last changes fastest.
Arguments:
- tokens: bfloat16 [1, 16, 8, 64, 512], P(None, 'gz', 'gy'), may hold values from -75 to 75
- w_qkv: bfloat16 [512, 1536], replicated, may hold values from -0.25 to 0.25
- w_out: bfloat16 [512, 512], replicated, may hold values from -0.25 to 0.25
- rel_bias: float32 [16, 5, 5, 5], replicated, may hold values from -4 to 4
- gain: float32 [512], replicated, may hold values from 0.5 to 1.5
Outputs:
- update: bfloat16 [1, 16, 8, 64, 512], P(None, 'gz', 'gy')
All inputs are finite; a program needn't handle non-finite values.
Results may differ from a plain program's by a relative error of at most 0.0079.
Values may be sent and summed in bfloat16 or wider, within the bound.
A program may use at most 128 MiB of HBM per device.

v0:
```python
import functools

import jax
import jax.numpy as jnp
from jax import lax
from jax.experimental import pallas as pl
from jax.experimental.pallas import tpu as pltpu
from jax.sharding import PartitionSpec as P

DILATION_DEPTH = 8


def shifted(block, axis, distance):
    devices = range(lax.axis_size(axis))
    route = [((i - distance) % len(devices), i) for i in devices]
    return lax.ppermute(block, axis, route)


def pick_rows(y_rows, per_row):
    chosen = 1
    for candidate in range(1, y_rows + 1):
        if y_rows % candidate == 0 and candidate * per_row <= 1024:
            chosen = candidate
    return chosen


def collect_planes(key_value, depth_stride, kernel_radius):
    axis_count = lax.axis_size("gz")
    received = {0: key_value}
    for offset in range(-kernel_radius, kernel_radius + 1):
        if offset != 0:
            distance = -offset * depth_stride % axis_count
            if distance == 0:
                received[offset] = key_value
            else:
                received[offset] = shifted(key_value, "gz", distance)
    return jnp.stack([received[offset] for offset in range(-kernel_radius, kernel_radius + 1)], 0)


def neighbourhood(queries, padded, bias_part):
    boxes, depth_planes, y_rows, x_cells, local_heads, head_dim = queries.shape
    kernel = padded.shape[0]
    kernel_radius = kernel // 2
    score_scale = float(head_dim) ** (-0.5)
    block_rows = pick_rows(y_rows, local_heads * x_cells)
    row_blocks = y_rows // block_rows
    block_count = boxes * depth_planes * row_blocks

    def tap_window(wide, tap_y):
        rows_part = wide[:, tap_y : tap_y + block_rows]
        return jnp.stack([rows_part[:, :, tap_x : tap_x + x_cells] for tap_x in range(kernel)], 1)

    def one_block(block_index):
        slab_index = block_index // row_blocks
        row_start = block_index % row_blocks * block_rows
        box_index = slab_index // depth_planes
        depth_plane_index = slab_index % depth_planes
        query_block = lax.dynamic_slice(
            queries,
            (box_index, depth_plane_index, row_start, 0, 0, 0),
            (1, 1, block_rows, x_cells, local_heads, head_dim),
        )[0, 0]
        pair_block = lax.dynamic_slice(
            padded,
            (0, box_index, depth_plane_index, row_start, 0, 0, 0, 0),
            (kernel, 1, 1, block_rows + 2 * kernel_radius, x_cells, local_heads, 2, head_dim),
        )[:, 0, 0]
        wide = jnp.concatenate(
            [
                pair_block[:, :, x_cells - kernel_radius :],
                pair_block,
                pair_block[:, :, :kernel_radius],
            ],
            axis=2,
        )
        score_parts = []
        for tap_y in range(kernel):
            window = tap_window(wide, tap_y)
            score_parts.append(
                jnp.einsum(
                    "yxhd,abyxhd->yhxab",
                    query_block,
                    window[..., 0, :],
                    preferred_element_type=jnp.float32,
                )
            )
        scores = jnp.stack(score_parts, 4) * score_scale + bias_part[None, :, None]
        row_max = jnp.max(scores, axis=(3, 4, 5), keepdims=True)
        exponent = jnp.exp(scores - row_max)
        weights = (exponent / jnp.sum(exponent, axis=(3, 4, 5), keepdims=True)).astype(jnp.bfloat16)
        mixed = jnp.zeros((block_rows, x_cells, local_heads, head_dim), jnp.float32)
        for tap_y in range(kernel):
            window = tap_window(wide, tap_y)
            mixed = mixed + jnp.einsum(
                "yhxab,abyxhd->yxhd",
                weights[:, :, :, :, tap_y],
                window[..., 1, :],
                preferred_element_type=jnp.float32,
            )
        return mixed.astype(jnp.bfloat16).reshape(block_rows, x_cells, local_heads * head_dim)

    block_out = lax.map(one_block, jnp.arange(block_count, dtype=jnp.int32))
    return block_out.reshape(boxes, depth_planes, y_rows, x_cells, local_heads * head_dim)


def body(tokens, w_qkv, w_out, rel_bias, gain):
    boxes, depth_planes, y_rows, x_cells, model_width = tokens.shape
    head_count = rel_bias.shape[0]
    kernel = rel_bias.shape[1]
    kernel_radius = kernel // 2
    head_dim = model_width // head_count
    depth_stride = DILATION_DEPTH // depth_planes
    projected = jnp.dot(
        tokens.reshape(-1, model_width), w_qkv, preferred_element_type=jnp.float32
    ).astype(jnp.bfloat16)
    projected = projected.reshape(boxes, depth_planes, y_rows, x_cells, 3 * model_width)
    exchanged = lax.all_to_all(projected, "gy", split_axis=4, concat_axis=2, tiled=True)
    local_heads = exchanged.shape[-1] // (3 * head_dim)
    unpacked = exchanged.reshape(exchanged.shape[:4] + (local_heads, 3, head_dim))
    queries = unpacked[..., 0, :]
    key_value = unpacked[..., 1:, :]
    plane_taps = collect_planes(key_value, depth_stride, kernel_radius)
    padded = jnp.concatenate(
        [plane_taps[:, :, :, -kernel_radius:], plane_taps, plane_taps[:, :, :, :kernel_radius]],
        axis=3,
    )
    head_start = lax.axis_index("gy") * local_heads
    bias_part = lax.dynamic_slice_in_dim(rel_bias, head_start, local_heads, 0)
    gathered = neighbourhood(queries, padded, bias_part)
    attended = lax.all_to_all(gathered, "gy", split_axis=2, concat_axis=4, tiled=True)
    projection = jnp.dot(
        attended.reshape(-1, model_width), w_out, preferred_element_type=jnp.float32
    )
    mean_sq = jnp.mean(projection * projection, axis=-1, keepdims=True)
    update = (projection * lax.rsqrt(mean_sq + 1e-06) * gain).astype(jnp.bfloat16)
    return update.reshape(boxes, depth_planes, y_rows, x_cells, model_width)


MASKED = -1e30
LOG2E = 1.4426950408889634
MESH_IDS = pl.DeviceIdType.MESH


def kernel_body(
    members, ring, half, tap_groups, radius, scale,
    tok_ref, wqkv_ref, wout_ref, bias_ref, gain_ref, out_ref,
    wqkv, wout, regrouped, halo_out, main_in, halo_in, bias_full, qkv, attended, returned,
    weight_sems, main_send, main_recv, halo_send, halo_recv, back_send, back_recv, local_sem,
):
    heads, kernel = bias_ref.shape[0], bias_ref.shape[2]
    rows, x_cells, width = tok_ref.shape[2:]
    chunk = x_cells // ring
    y_total = rows * ring
    head_dim = width // heads
    lanes = y_total * chunk
    groups = width // lanes
    per_group = lanes // head_dim
    halo_rows = halo_in.shape[1]
    halo_slots = halo_rows // rows
    keys = members * lanes + members * ring * halo_rows
    gz, gy = lax.axis_index("gz"), lax.axis_index("gy")
    mine, base = gz // half, gz % half
    slot = mine * ring + gy
    partners = [(dm, dg) for dm in reversed(range(members)) for dg in range(ring) if (dm, dg) != (0, 0)]

    def member(dm):
        return lax.rem(mine + dm, members)

    def ring_place(dg):
        return lax.rem(gy + dg, ring)

    def target(dm, dg):
        return (base + member(dm) * half, ring_place(dg))

    barrier = pltpu.get_barrier_semaphore()
    for dm, dg in partners:
        pl.semaphore_signal(barrier, inc=1, device_id=target(dm, dg), device_id_type=MESH_IDS)
    load_qkv = pltpu.make_async_copy(wqkv_ref, wqkv, weight_sems.at[0])
    load_out = pltpu.make_async_copy(wout_ref, wout, weight_sems.at[1])
    load_qkv.start()
    load_out.start()

    count = ring * halo_rows
    line = lax.broadcasted_iota(jnp.int32, (count, rows * x_cells), 0)
    source = lax.broadcasted_iota(jnp.int32, (count, rows * x_cells), 1)
    place, within = line // halo_rows, line % halo_rows
    row, column = within // halo_slots, within % halo_slots
    column_x = place * chunk + jnp.where(column < radius, column - radius, column + chunk - radius)
    wanted = row * x_cells + (column_x + x_cells) % x_cells
    pick = jnp.where((source == wanted) & (column < 2 * radius), 1.0, 0.0).astype(jnp.bfloat16)
    for plane in range(members):
        flat = tok_ref[0, plane].reshape(rows * x_cells, width)
        picked = jnp.dot(pick, flat, preferred_element_type=jnp.float32).astype(jnp.bfloat16)
        halo_out[plane] = picked.reshape(ring, halo_rows, width)

    pl.semaphore_wait(barrier, len(partners))
    sends = []
    for dm, dg in partners:
        index = dm * ring + dg
        columns = pl.ds(pl.multiple_of(ring_place(dg) * chunk, chunk), chunk)
        sends.append(
            pltpu.make_async_remote_copy(
                src_ref=tok_ref.at[0, member(dm), :, columns, :],
                dst_ref=main_in.at[slot],
                send_sem=main_send.at[index],
                recv_sem=main_recv.at[index],
                device_id=target(dm, dg),
                device_id_type=MESH_IDS,
            )
        )
        sends.append(
            pltpu.make_async_remote_copy(
                src_ref=halo_out.at[member(dm), ring_place(dg)],
                dst_ref=halo_in.at[slot],
                send_sem=halo_send.at[index],
                recv_sem=halo_recv.at[index],
                device_id=target(dm, dg),
                device_id_type=MESH_IDS,
            )
        )
    for copy in sends:
        copy.start()
    own_columns = pl.ds(pl.multiple_of(gy * chunk, chunk), chunk)
    main_in[slot] = tok_ref[0, mine, :, own_columns, :]
    halo_in[slot] = halo_out[mine, gy]

    x_query = lax.broadcasted_iota(jnp.int32, (chunk, lanes), 0)
    lane = lax.broadcasted_iota(jnp.int32, (chunk, lanes), 1)

    def tap_map(y_key, x_key, valid):
        tap_y = (y_key + radius) % y_total
        tap_x = x_key - x_query + radius
        inside = valid & (tap_y < kernel) & (tap_x >= 0) & (tap_x < kernel)
        return jnp.where(inside, tap_y * kernel + tap_x, -1)

    main_taps = tap_map(lane // chunk, lane % chunk, lane >= 0)
    halo_lane = lane % (y_total * halo_slots)
    halo_column = halo_lane % halo_slots
    halo_x = jnp.where(halo_column < radius, halo_column - radius, halo_column + chunk - radius)
    halo_taps = tap_map(halo_lane // halo_slots, halo_x, halo_column < 2 * radius)
    first_half = lane < y_total * halo_slots

    def bias_of_head(head, carry):
        mains, halos = [], []
        for taps in tap_groups:
            parts = [bias_ref[head, i] for i in taps]
            top = functools.reduce(jnp.maximum, parts)
            merged = (top + jnp.log(sum(jnp.exp(part - top) for part in parts))) * LOG2E
            main = jnp.full((chunk, lanes), MASKED, jnp.float32)
            halo = main
            for tap_x in range(kernel):
                spread = jnp.broadcast_to(merged[:, tap_x : tap_x + 1], (kernel, lanes))
                for tap_y in range(kernel):
                    value = spread[tap_y : tap_y + 1, :]
                    main = jnp.where(main_taps == tap_y * kernel + tap_x, value, main)
                    halo = jnp.where(halo_taps == tap_y * kernel + tap_x, value, halo)
            mains.append(main)
            halos.append(halo)
        for y in range(y_total):
            here = pl.ds(y * chunk, chunk)
            turned = [pltpu.roll(main, y * chunk, 1) if y else main for main in mains]
            turned_halo = [pltpu.roll(halo, y * halo_slots, 1) if y else halo for halo in halos]
            for plane in range(2):
                bias_full[head, plane, here, 0:lanes] = turned[plane]
                bias_full[head, plane, here, lanes : 2 * lanes] = turned[1 - plane]
                bias_full[head, plane, here, 2 * lanes : 3 * lanes] = jnp.where(
                    first_half, turned_halo[plane], turned_halo[1 - plane]
                )
        return carry

    lax.fori_loop(0, heads, bias_of_head, 0)

    span = 3 * lanes
    before = lax.broadcasted_iota(jnp.int32, (span, span), 0)
    after = lax.broadcasted_iota(jnp.int32, (span, span), 1)
    origin = (after % lanes) // head_dim * (3 * head_dim) + after // lanes * head_dim + after % head_dim
    order = jnp.where(before == origin, 1.0, 0.0).astype(jnp.bfloat16)
    load_qkv.wait()
    for group in range(groups):
        regrouped[group] = jnp.dot(
            wqkv[:, group * span : (group + 1) * span], order, preferred_element_type=jnp.float32
        ).astype(jnp.bfloat16)

    for copy in sends:
        copy.wait_recv()
    main = main_in[...].reshape(members * lanes, width)
    halo = halo_in[...].reshape(members * ring * halo_rows, width)
    for group in range(groups):
        weight = regrouped[group]
        qkv[group, 0 : members * lanes] = jnp.dot(
            main, weight, preferred_element_type=jnp.float32
        ).astype(jnp.bfloat16)
        qkv[group, members * lanes : keys] = jnp.dot(
            halo, weight, preferred_element_type=jnp.float32
        ).astype(jnp.bfloat16)

    owner = lax.broadcasted_iota(jnp.int32, (lanes, lanes), 1) // head_dim
    ones = jnp.ones((keys, lanes), jnp.bfloat16)
    load_out.wait()
    backs = []
    for dm in reversed(range(members)):
        plane = member(dm)
        query_rows = pl.ds(pl.multiple_of(plane * lanes, lanes), lanes)

        def attend(group, carry):
            query = qkv[group, query_rows, 0:lanes]
            key = qkv[group, :, lanes : 2 * lanes]
            value = jnp.concatenate([qkv[group, :, 2 * lanes : 3 * lanes], ones], axis=1)
            mixed = jnp.zeros((lanes, lanes), jnp.float32)
            for within in range(per_group):
                own = jnp.where(owner == within, query, jnp.zeros_like(query))
                scores = lax.dot_general(
                    own, key, (((1,), (1,)), ((), ())), preferred_element_type=jnp.float32
                )
                scores = scores * (scale * LOG2E) + bias_full[group * per_group + within, plane]
                row_max = jnp.max(scores, axis=1, keepdims=True)
                weights = jnp.exp2(scores - row_max).astype(jnp.bfloat16)
                both = jnp.dot(weights, value, preferred_element_type=jnp.float32)
                mixed = jnp.where(owner == within, both[:, :lanes] / both[:, lanes:], mixed)
            attended[group] = mixed.astype(jnp.bfloat16)
            return carry

        lax.fori_loop(0, groups, attend, 0)
        joined = jnp.concatenate([attended[group] for group in range(groups)], axis=1)
        projection = jnp.dot(joined, wout[...], preferred_element_type=jnp.float32)
        mean_sq = jnp.mean(projection * projection, axis=-1, keepdims=True)
        update = (projection * lax.rsqrt(mean_sq + 1e-06) * gain_ref[...]).astype(jnp.bfloat16)
        returned[dm] = update.reshape(ring, rows, chunk, width)
        for dg in range(ring):
            index = dm * ring + dg
            landing = out_ref.at[0, mine, :, own_columns, :]
            if (dm, dg) == (0, 0):
                own_copy = pltpu.make_async_copy(returned.at[dm, gy], landing, local_sem)
                own_copy.start()
            else:
                back = pltpu.make_async_remote_copy(
                    src_ref=returned.at[dm, ring_place(dg)],
                    dst_ref=landing,
                    send_sem=back_send.at[index],
                    recv_sem=back_recv.at[index],
                    device_id=target(dm, dg),
                    device_id_type=MESH_IDS,
                )
                back.start()
                backs.append(back)
    for copy in sends:
        copy.wait_send()
    for copy in backs:
        copy.wait()
    own_copy.wait()


def pair_plan(mesh_shape, depth_total, shapes):
    boxes, planes, rows, x_cells, width, heads, kernel = shapes
    depth_devices, ring = mesh_shape
    radius = kernel // 2
    head_dim = width // heads
    offsets = [DILATION_DEPTH * (i - radius) % depth_total for i in range(kernel)]
    halo_slots = 8
    if boxes != 1 or planes != 2 or depth_total != 2 * DILATION_DEPTH or depth_devices % 2:
        return None
    if x_cells % ring or kernel % 2 == 0:
        return None
    chunk, y_total = x_cells // ring, rows * ring
    lanes = chunk * y_total
    if lanes != 128 or chunk % 16 or kernel > y_total or 2 * y_total * halo_slots != lanes:
        return None
    if rows * halo_slots % 16 or 2 * radius > halo_slots or lanes % head_dim or width % lanes:
        return None
    return halo_slots, [[i for i in range(kernel) if offsets[i] == p * DILATION_DEPTH] for p in range(2)]


def fused(plan, depth_devices, ring, tokens, w_qkv, w_out, rel_bias, gain):
    halo_slots, tap_groups = plan
    _, planes, rows, x_cells, width = tokens.shape
    heads, kernel = rel_bias.shape[0], rel_bias.shape[1]
    chunk = x_cells // ring
    lanes = chunk * rows * ring
    groups = width // lanes
    halo_rows = rows * halo_slots
    members, slots = planes, planes * ring
    keys = 3 * lanes
    vmem = pl.BlockSpec(memory_space=pltpu.VMEM)
    anywhere = pl.BlockSpec(memory_space=pl.ANY)
    body_of = functools.partial(
        kernel_body, members, ring, depth_devices // 2, tap_groups, kernel // 2,
        float(width // heads) ** (-0.5),
    )
    dma = pltpu.SemaphoreType.DMA
    return pl.pallas_call(
        body_of,
        out_shape=jax.ShapeDtypeStruct(tokens.shape, jnp.bfloat16),
        in_specs=[vmem, anywhere, anywhere, vmem, vmem],
        out_specs=anywhere,
        scratch_shapes=[
            pltpu.VMEM(w_qkv.shape, jnp.bfloat16),
            pltpu.VMEM(w_out.shape, jnp.bfloat16),
            pltpu.VMEM((groups, width, 3 * lanes), jnp.bfloat16),
            pltpu.VMEM((members, ring, halo_rows, width), jnp.bfloat16),
            pltpu.VMEM((slots, rows, chunk, width), jnp.bfloat16),
            pltpu.VMEM((slots, halo_rows, width), jnp.bfloat16),
            pltpu.VMEM((heads, members, lanes, keys), jnp.float32),
            pltpu.VMEM((groups, keys, 3 * lanes), jnp.bfloat16),
            pltpu.VMEM((groups, lanes, lanes), jnp.bfloat16),
            pltpu.VMEM((members, ring, rows, chunk, width), jnp.bfloat16),
            dma((2,)), dma((slots,)), dma((slots,)), dma((slots,)), dma((slots,)),
            dma((slots,)), dma((slots,)), dma,
        ],
        compiler_params=pltpu.CompilerParams(
            collective_id=0, has_side_effects=True, vmem_limit_bytes=40 * 1024 * 1024
        ),
    )(tokens, w_qkv, w_out, rel_bias, gain.reshape(1, width))


def solution(mesh):
    depth_devices, ring = mesh.shape["gz"], mesh.shape["gy"]

    def chosen(tokens, w_qkv, w_out, rel_bias, gain):
        shapes = tokens.shape + rel_bias.shape[:2]
        plan = pair_plan((depth_devices, ring), tokens.shape[1] * depth_devices, shapes)
        if plan is None:
            return body(tokens, w_qkv, w_out, rel_bias, gain)
        return fused(plan, depth_devices, ring, tokens, w_qkv, w_out, rel_bias, gain)

    in_specs = (P(None, "gz", "gy", None, None), P(), P(), P(), P())
    out_specs = P(None, "gz", "gy", None, None)
    return jax.shard_map(chosen, mesh=mesh, in_specs=in_specs, out_specs=out_specs, check_vma=False)
```

profile of v0, /device:TPU:0, one launch (start us, length us, event | category | flops | bytes accessed | tf_op | source)
XLA Modules:
  0.0 33.0 jit_solution(17621590179167774915)
XLA Ops:
  0.0 1.1 %copy.6.bias_ref = f32[16,5,5,5]{3,2,1,0:T(8,128)S(1)} copy(f32[16,5,5,5]{0,3,2,1:T(8,128)} %param.8) | data formatting | bytes 16000 | tf_op args[3]
  1.1 0.0 copy-start
  1.1 1.4 %copy-done = bf16[512,1536]{1,0:T(8,128)(2,1)S(1)} copy-done((bf16[512,1536]{1,0:T(8,128)(2,1)S(1)}, bf16[512,1536]{1,0:T(8,128)(2,1)}, u32[]{:S(2)}) %copy-start) | copy-done | bytes 1572888
  2.5 0.0 copy-start.1
  2.5 1.0 %copy-done.1 = bf16[512,512]{1,0:T(8,128)(2,1)S(1)} copy-done((bf16[512,512]{1,0:T(8,128)(2,1)S(1)}, bf16[512,512]{1,0:T(8,128)(2,1)}, u32[]{:S(2)}) %copy-start.1) | copy-done | bytes 524312
  3.6 0.0 copy-start.2
  3.6 0.9 %copy-done.2 = bf16[1,2,2,64,512]{4,3,2,1,0:T(8,128)(2,1)S(1)} copy-done((bf16[1,2,2,64,512]{4,3,2,1,0:T(8,128)(2,1)S(1)}, bf16[1,2,2,64,512]{4,3,2,1,0:T(8,128)(2,1)}, u32[]{:S(2)}) %copy-start.2) | copy-done | bytes 262168
  4.5 0.0 copy-start.3
  4.5 0.7 %copy-done.3 = f32[512]{0:T(512)S(1)} copy-done((f32[512]{0:T(512)S(1)}, f32[512]{0:T(512)}, u32[]{:S(2)}) %copy-start.3) | copy-done | bytes 2072
  5.2 27.1 %shard_map.55 = bf16[1,2,2,64,512]{4,3,2,1,0:T(8,128)(2,1)S(1)} custom-call(bf16[1,2,2,64,512]{4,3,2,1,0:T(8,128)(2,1)S(1)} %copy-done.2, bf16[512,1536]{1,0:T(8,128)(2,1)S(1)} %copy-done, bf16[512,512]{1,0:T(8,128)(2,1)S(1)} %copy-done.1, f32[16,5,5,5]{3,2,1,0:T(8,128)S(1)} %copy.6.bias_ref, f32[1,512]{1,0:T(1,128)S(1)} %bitcast.1), custom_call_target="tpu_custom_call" | custom-call | tf_op jit(solution)/shard_map/pallas_call | solution.py:390
  32.3 0.7 %copy.8 = bf16[1,2,2,64,512]{4,3,2,1,0:T(8,128)(2,1)} copy(bf16[1,2,2,64,512]{4,3,2,1,0:T(8,128)(2,1)S(1)} %shard_map.55) | data formatting | bytes 524288
Async XLA Ops:
  1.1 1.4 %copy-start = (bf16[512,1536]{1,0:T(8,128)(2,1)S(1)}, bf16[512,1536]{1,0:T(8,128)(2,1)}, u32[]{:S(2)}) copy-start(bf16[512,1536]{1,0:T(8,128)(2,1)} %wqkv_ref.1) | copy-start | bytes 4718596
  2.5 1.0 %copy-start.1 = (bf16[512,512]{1,0:T(8,128)(2,1)S(1)}, bf16[512,512]{1,0:T(8,128)(2,1)}, u32[]{:S(2)}) copy-start(bf16[512,512]{1,0:T(8,128)(2,1)} %wout_ref.1) | copy-start | bytes 1572868
  3.6 0.9 %copy-start.2 = (bf16[1,2,2,64,512]{4,3,2,1,0:T(8,128)(2,1)S(1)}, bf16[1,2,2,64,512]{4,3,2,1,0:T(8,128)(2,1)}, u32[]{:S(2)}) copy-start(bf16[1,2,2,64,512]{4,3,2,1,0:T(8,128)(2,1)} %tok_ref.1) | copy-start | bytes 786436
  4.5 0.7 %copy-start.3 = (f32[512]{0:T(512)S(1)}, f32[512]{0:T(512)}, u32[]{:S(2)}) copy-start(f32[512]{0:T(512)} %param.9) | copy-start | bytes 6148
where the time goes:
time: 33.3 us; the launch traced here: 33 us
  Pallas kernels  27.1 us (81%)
  local copies, waits for them, and re-layouts  5.9 us (18%)
    pallas_call x1, Pallas kernels, fused(): pl.pallas_call(body_of, out_shape=jax.ShapeDtypeStruct(tokens.shape, jnp....  27.1 us
    unnamed x10, local copies, waits for them, and re-layouts  5.9 us

commit v1 on v0

--- a/solution.py
+++ b/solution.py
@@ -136,6 +136,7 @@
     return update.reshape(boxes, depth_planes, y_rows, x_cells, model_width)
 
 
+SPLITS = 1
 MASKED = -1e30
 LOG2E = 1.4426950408889634
 MESH_IDS = pl.DeviceIdType.MESH
@@ -143,11 +144,11 @@
 
 def kernel_body(
     members, ring, half, tap_groups, radius, scale,
-    tok_ref, wqkv_ref, wout_ref, bias_ref, gain_ref, out_ref,
-    wqkv, wout, regrouped, halo_out, main_in, halo_in, bias_full, qkv, attended, returned,
-    weight_sems, main_send, main_recv, halo_send, halo_recv, back_send, back_recv, local_sem,
+    tok_hbm, wqkv_ref, wout_ref, bias_hbm, gain_hbm, out_ref,
+    tok_ref, bias_ref, gain_ref, wqkv, wout, regrouped, halo_out, main_in, halo_in, bias_full, qkv, returned,
+    weight_sems, main_send, main_recv, halo_send, halo_recv, back_send, back_recv,
 ):
-    heads, kernel = bias_ref.shape[0], bias_ref.shape[2]
+    kernel, heads = bias_ref.shape[0], bias_ref.shape[3]
     rows, x_cells, width = tok_ref.shape[2:]
     chunk = x_cells // ring
     y_total = rows * ring
@@ -155,9 +156,11 @@
     lanes = y_total * chunk
     groups = width // lanes
     per_group = lanes // head_dim
-    halo_rows = halo_in.shape[1]
-    halo_slots = halo_rows // rows
-    keys = members * lanes + members * ring * halo_rows
+    halo_rows, half_width = halo_in.shape[1:]
+    halo_slots = 2 * radius
+    halo_cells = rows * halo_slots
+    halo_keys = ring * halo_cells
+    keys = 3 * lanes
     gz, gy = lax.axis_index("gz"), lax.axis_index("gy")
     mine, base = gz // half, gz % half
     slot = mine * ring + gy
@@ -175,23 +178,16 @@
     barrier = pltpu.get_barrier_semaphore()
     for dm, dg in partners:
         pl.semaphore_signal(barrier, inc=1, device_id=target(dm, dg), device_id_type=MESH_IDS)
+    load_tokens = pltpu.make_async_copy(tok_hbm, tok_ref, weight_sems.at[2])
+    load_bias = pltpu.make_async_copy(bias_hbm, bias_ref, weight_sems.at[3])
+    load_gain = pltpu.make_async_copy(gain_hbm, gain_ref, weight_sems.at[4])
+    load_tokens.start()
+    load_bias.start()
     load_qkv = pltpu.make_async_copy(wqkv_ref, wqkv, weight_sems.at[0])
     load_out = pltpu.make_async_copy(wout_ref, wout, weight_sems.at[1])
     load_qkv.start()
     load_out.start()
-
-    count = ring * halo_rows
-    line = lax.broadcasted_iota(jnp.int32, (count, rows * x_cells), 0)
-    source = lax.broadcasted_iota(jnp.int32, (count, rows * x_cells), 1)
-    place, within = line // halo_rows, line % halo_rows
-    row, column = within // halo_slots, within % halo_slots
-    column_x = place * chunk + jnp.where(column < radius, column - radius, column + chunk - radius)
-    wanted = row * x_cells + (column_x + x_cells) % x_cells
-    pick = jnp.where((source == wanted) & (column < 2 * radius), 1.0, 0.0).astype(jnp.bfloat16)
-    for plane in range(members):
-        flat = tok_ref[0, plane].reshape(rows * x_cells, width)
-        picked = jnp.dot(pick, flat, preferred_element_type=jnp.float32).astype(jnp.bfloat16)
-        halo_out[plane] = picked.reshape(ring, halo_rows, width)
+    load_gain.start()
 
     pl.semaphore_wait(barrier, len(partners))
     sends = []
@@ -200,7 +196,7 @@
         columns = pl.ds(pl.multiple_of(ring_place(dg) * chunk, chunk), chunk)
         sends.append(
             pltpu.make_async_remote_copy(
-                src_ref=tok_ref.at[0, member(dm), :, columns, :],
+                src_ref=tok_hbm.at[0, member(dm), :, columns, :],
                 dst_ref=main_in.at[slot],
                 send_sem=main_send.at[index],
                 recv_sem=main_recv.at[index],
@@ -208,6 +204,26 @@
                 device_id_type=MESH_IDS,
             )
         )
+        sends[-1].start()
+
+    count = ring * halo_rows
+    line = lax.broadcasted_iota(jnp.int32, (count, rows * x_cells), 0)
+    source = lax.broadcasted_iota(jnp.int32, (count, rows * x_cells), 1)
+    place, within = line // halo_rows, line % halo_cells
+    row, column = within // halo_slots, within % halo_slots
+    column_x = place * chunk + jnp.where(column < radius, column - radius, column + chunk - radius)
+    wanted = row * x_cells + (column_x + x_cells) % x_cells
+    pick = jnp.where(source == wanted, 1.0, 0.0).astype(jnp.bfloat16)
+    upper = lax.broadcasted_iota(jnp.int32, (count, half_width), 0) % halo_rows < halo_cells
+    load_tokens.wait()
+    for plane in range(members):
+        flat = tok_ref[0, plane].reshape(rows * x_cells, width)
+        picked = jnp.dot(pick, flat, preferred_element_type=jnp.float32)
+        folded = jnp.where(upper, picked[:, :half_width], picked[:, half_width:])
+        halo_out[plane] = folded.astype(jnp.bfloat16).reshape(ring, halo_rows, half_width)
+
+    for dm, dg in partners:
+        index = dm * ring + dg
         sends.append(
             pltpu.make_async_remote_copy(
                 src_ref=halo_out.at[member(dm), ring_place(dg)],
@@ -218,8 +234,7 @@
                 device_id_type=MESH_IDS,
             )
         )
-    for copy in sends:
-        copy.start()
+        sends[-1].start()
     own_columns = pl.ds(pl.multiple_of(gy * chunk, chunk), chunk)
     main_in[slot] = tok_ref[0, mine, :, own_columns, :]
     halo_in[slot] = halo_out[mine, gy]
@@ -237,21 +252,27 @@
     halo_lane = lane % (y_total * halo_slots)
     halo_column = halo_lane % halo_slots
     halo_x = jnp.where(halo_column < radius, halo_column - radius, halo_column + chunk - radius)
-    halo_taps = tap_map(halo_lane // halo_slots, halo_x, halo_column < 2 * radius)
-    first_half = lane < y_total * halo_slots
+    halo_taps = tap_map(halo_lane // halo_slots, halo_x, lane >= 0)
+    halo_plane = lane // halo_keys
+
+    load_bias.wait()
+    merged_bias = []
+    for taps in tap_groups:
+        parts = [bias_ref[i] for i in taps]
+        top = functools.reduce(jnp.maximum, parts)
+        merged_bias.append((top + jnp.log(sum(jnp.exp(part - top) for part in parts))) * LOG2E)
+    head_lane = lax.broadcasted_iota(jnp.int32, (kernel, kernel, heads), 2)
 
     def bias_of_head(head, carry):
         mains, halos = [], []
-        for taps in tap_groups:
-            parts = [bias_ref[head, i] for i in taps]
-            top = functools.reduce(jnp.maximum, parts)
-            merged = (top + jnp.log(sum(jnp.exp(part - top) for part in parts))) * LOG2E
+        for merged in merged_bias:
+            column = jnp.sum(jnp.where(head_lane == head, merged, 0.0), axis=2, keepdims=True)
+            spread = jnp.broadcast_to(column, (kernel, kernel, lanes))
             main = jnp.full((chunk, lanes), MASKED, jnp.float32)
             halo = main
-            for tap_x in range(kernel):
-                spread = jnp.broadcast_to(merged[:, tap_x : tap_x + 1], (kernel, lanes))
-                for tap_y in range(kernel):
-                    value = spread[tap_y : tap_y + 1, :]
+            for tap_y in range(kernel):
+                for tap_x in range(kernel):
+                    value = spread[tap_y, tap_x : tap_x + 1, :]
                     main = jnp.where(main_taps == tap_y * kernel + tap_x, value, main)
                     halo = jnp.where(halo_taps == tap_y * kernel + tap_x, value, halo)
             mains.append(main)
@@ -264,7 +285,9 @@
                 bias_full[head, plane, here, 0:lanes] = turned[plane]
                 bias_full[head, plane, here, lanes : 2 * lanes] = turned[1 - plane]
                 bias_full[head, plane, here, 2 * lanes : 3 * lanes] = jnp.where(
-                    first_half, turned_halo[plane], turned_halo[1 - plane]
+                    halo_plane == 0,
+                    turned_halo[plane],
+                    jnp.where(halo_plane == 1, turned_halo[1 - plane], MASKED),
                 )
         return carry
 
@@ -281,73 +304,114 @@
             wqkv[:, group * span : (group + 1) * span], order, preferred_element_type=jnp.float32
         ).astype(jnp.bfloat16)
 
-    for copy in sends:
-        copy.wait_recv()
-    main = main_in[...].reshape(members * lanes, width)
-    halo = halo_in[...].reshape(members * ring * halo_rows, width)
+    def project(dm):
+        for copy, (sent_dm, _) in zip(sends, partners + partners):
+            if sent_dm == dm:
+                copy.wait_recv()
+        plane = member(dm)
+        slots = pl.ds(plane * ring, ring)
+        main_rows = pl.ds(pl.multiple_of(plane * lanes, lanes), lanes)
+        halo_keys_at = pl.ds(pl.multiple_of(members * lanes + plane * halo_keys, halo_keys), halo_keys)
+        main = main_in[slots].reshape(lanes, width)
+        folded = halo_in[slots].reshape(ring * halo_rows, half_width)
+        for group in range(groups):
+            weight = regrouped[group]
+            qkv[group, main_rows] = jnp.dot(
+                main, weight, preferred_element_type=jnp.float32
+            ).astype(jnp.bfloat16)
+            first = jnp.dot(folded, weight[:half_width], preferred_element_type=jnp.float32)
+            second = jnp.dot(folded, weight[half_width:], preferred_element_type=jnp.float32)
+            both = (
+                first.reshape(ring, halo_rows, span)[:, :halo_cells]
+                + second.reshape(ring, halo_rows, span)[:, halo_cells:]
+            )
+            qkv[group, halo_keys_at] = both.reshape(halo_keys, span).astype(jnp.bfloat16)
+
+    unused = keys - members * (lanes + halo_keys)
     for group in range(groups):
-        weight = regrouped[group]
-        qkv[group, 0 : members * lanes] = jnp.dot(
-            main, weight, preferred_element_type=jnp.float32
-        ).astype(jnp.bfloat16)
-        qkv[group, members * lanes : keys] = jnp.dot(
-            halo, weight, preferred_element_type=jnp.float32
-        ).astype(jnp.bfloat16)
-
-    owner = lax.broadcasted_iota(jnp.int32, (lanes, lanes), 1) // head_dim
+        qkv[group, keys - unused : keys] = jnp.zeros((unused, span), jnp.bfloat16)
+    for dm in range(members):
+        project(dm)
+
+    block = lanes // SPLITS
+    places = ring // SPLITS
+    owner = lax.broadcasted_iota(jnp.int32, (block, lanes), 1) // head_dim
     ones = jnp.ones((keys, lanes), jnp.bfloat16)
     load_out.wait()
+    load_gain.wait()
     backs = []
-    for dm in reversed(range(members)):
+    landing = out_ref.at[0, mine, :, own_columns, :]
+    for dm, part in [(dm, part) for dm in reversed(range(members)) for part in range(SPLITS)]:
         plane = member(dm)
-        query_rows = pl.ds(pl.multiple_of(plane * lanes, lanes), lanes)
-
-        def attend(group, carry):
+        first_row = part * block
+        query_rows = pl.ds(pl.multiple_of(plane * lanes + first_row, block), block)
+
+        def attend(group):
             query = qkv[group, query_rows, 0:lanes]
             key = qkv[group, :, lanes : 2 * lanes]
             value = jnp.concatenate([qkv[group, :, 2 * lanes : 3 * lanes], ones], axis=1)
-            mixed = jnp.zeros((lanes, lanes), jnp.float32)
-            for within in range(per_group):
-                own = jnp.where(owner == within, query, jnp.zeros_like(query))
-                scores = lax.dot_general(
-                    own, key, (((1,), (1,)), ((), ())), preferred_element_type=jnp.float32
-                )
-                scores = scores * (scale * LOG2E) + bias_full[group * per_group + within, plane]
-                row_max = jnp.max(scores, axis=1, keepdims=True)
-                weights = jnp.exp2(scores - row_max).astype(jnp.bfloat16)
-                both = jnp.dot(weights, value, preferred_element_type=jnp.float32)
-                mixed = jnp.where(owner == within, both[:, :lanes] / both[:, lanes:], mixed)
-            attended[group] = mixed.astype(jnp.bfloat16)
-            return carry
-
-        lax.fori_loop(0, groups, attend, 0)
-        joined = jnp.concatenate([attended[group] for group in range(groups)], axis=1)
+            own = jnp.concatenate(
+                [jnp.where(owner == within, query, jnp.zeros_like(query)) for within in range(per_group)], axis=0
+            )
+            scores = lax.dot_general(
+                own, key, (((1,), (1,)), ((), ())), preferred_element_type=jnp.float32
+            )
+            bias = bias_full[
+                group * per_group : (group + 1) * per_group, plane, first_row : first_row + block
+            ]
+            scores = scores * (scale * LOG2E) + bias.reshape(per_group * block, keys)
+            row_max = jnp.max(scores, axis=1, keepdims=True)
+            weights = jnp.exp2(scores - row_max).astype(jnp.bfloat16)
+            both = jnp.dot(weights, value, preferred_element_type=jnp.float32)
+            both = both.reshape(per_group, block, 2 * lanes)
+            mixed, total = both[0, :, :lanes], both[0, :, lanes:]
+            for within in range(1, per_group):
+                mixed = jnp.where(owner == within, both[within, :, :lanes], mixed)
+                total = jnp.where(owner == within, both[within, :, lanes:], total)
+            return (mixed / total).astype(jnp.bfloat16)
+
+        joined = jnp.concatenate([attend(group) for group in range(groups)], axis=1)
         projection = jnp.dot(joined, wout[...], preferred_element_type=jnp.float32)
         mean_sq = jnp.mean(projection * projection, axis=-1, keepdims=True)
         update = (projection * lax.rsqrt(mean_sq + 1e-06) * gain_ref[...]).astype(jnp.bfloat16)
-        returned[dm] = update.reshape(ring, rows, chunk, width)
-        for dg in range(ring):
-            index = dm * ring + dg
-            landing = out_ref.at[0, mine, :, own_columns, :]
-            if (dm, dg) == (0, 0):
-                own_copy = pltpu.make_async_copy(returned.at[dm, gy], landing, local_sem)
-                own_copy.start()
+        finished = update.reshape(places, rows, chunk, width)
+        returned[dm, part * places : (part + 1) * places] = finished
+        for place in range(part * places, (part + 1) * places):
+            going = returned.at[dm, place]
+            if dm == 0:
+                @pl.when(place == gy)
+                def _():
+                    out_ref[0, mine, :, own_columns, :] = returned[dm, place]
+
+                @pl.when(place != gy)
+                def _():
+                    pltpu.make_async_remote_copy(
+                        src_ref=going, dst_ref=landing,
+                        send_sem=back_send.at[place], recv_sem=back_recv.at[gy],
+                        device_id=(gz, place), device_id_type=MESH_IDS,
+                    ).start()
             else:
                 back = pltpu.make_async_remote_copy(
-                    src_ref=returned.at[dm, ring_place(dg)],
-                    dst_ref=landing,
-                    send_sem=back_send.at[index],
-                    recv_sem=back_recv.at[index],
-                    device_id=target(dm, dg),
-                    device_id_type=MESH_IDS,
+                    src_ref=going, dst_ref=landing,
+                    send_sem=back_send.at[ring + place], recv_sem=back_recv.at[ring + gy],
+                    device_id=(base + plane * half, place), device_id_type=MESH_IDS,
                 )
                 back.start()
-                backs.append(back)
     for copy in sends:
         copy.wait_send()
-    for copy in backs:
-        copy.wait()
-    own_copy.wait()
+    for dm in reversed(range(members)):
+        for place in range(ring):
+            def finish():
+                pltpu.make_async_remote_copy(
+                    src_ref=returned.at[dm, place], dst_ref=landing,
+                    send_sem=back_send.at[dm * ring + place], recv_sem=back_recv.at[dm * ring + place],
+                    device_id=(base + member(dm) * half, place), device_id_type=MESH_IDS,
+                ).wait()
+
+            if dm:
+                finish()
+            else:
+                pl.when(place != gy)(finish)
 
 
 def pair_plan(mesh_shape, depth_total, shapes):
@@ -356,16 +420,16 @@
     radius = kernel // 2
     head_dim = width // heads
     offsets = [DILATION_DEPTH * (i - radius) % depth_total for i in range(kernel)]
-    halo_slots = 8
+    halo_slots = 2 * radius
     if boxes != 1 or planes != 2 or depth_total != 2 * DILATION_DEPTH or depth_devices % 2:
         return None
     if x_cells % ring or kernel % 2 == 0:
         return None
     chunk, y_total = x_cells // ring, rows * ring
     lanes = chunk * y_total
-    if lanes != 128 or chunk % 16 or kernel > y_total or 2 * y_total * halo_slots != lanes:
+    if lanes != 128 or chunk % 16 or kernel > y_total or 2 * y_total * halo_slots > lanes:
         return None
-    if rows * halo_slots % 16 or 2 * radius > halo_slots or lanes % head_dim or width % lanes:
+    if rows * halo_slots != 8 or lanes % head_dim or width % (2 * lanes) or ring % SPLITS:
         return None
     return halo_slots, [[i for i in range(kernel) if offsets[i] == p * DILATION_DEPTH] for p in range(2)]
 
@@ -377,11 +441,11 @@
     chunk = x_cells // ring
     lanes = chunk * rows * ring
     groups = width // lanes
-    halo_rows = rows * halo_slots
+    halo_rows = 2 * rows * halo_slots
     members, slots = planes, planes * ring
     keys = 3 * lanes
     vmem = pl.BlockSpec(memory_space=pltpu.VMEM)
-    anywhere = pl.BlockSpec(memory_space=pl.ANY)
+    hbm = pl.BlockSpec(memory_space=pltpu.HBM)
     body_of = functools.partial(
         kernel_body, members, ring, depth_devices // 2, tap_groups, kernel // 2,
         float(width // heads) ** (-0.5),
@@ -390,26 +454,28 @@
     return pl.pallas_call(
         body_of,
         out_shape=jax.ShapeDtypeStruct(tokens.shape, jnp.bfloat16),
-        in_specs=[vmem, anywhere, anywhere, vmem, vmem],
-        out_specs=anywhere,
+        in_specs=[hbm] * 5,
+        out_specs=vmem,
         scratch_shapes=[
+            pltpu.VMEM(tokens.shape, jnp.bfloat16),
+            pltpu.VMEM(rel_bias.shape[1:] + (heads,), jnp.float32),
+            pltpu.VMEM((1, width), jnp.float32),
             pltpu.VMEM(w_qkv.shape, jnp.bfloat16),
             pltpu.VMEM(w_out.shape, jnp.bfloat16),
             pltpu.VMEM((groups, width, 3 * lanes), jnp.bfloat16),
-            pltpu.VMEM((members, ring, halo_rows, width), jnp.bfloat16),
+            pltpu.VMEM((members, ring, halo_rows, width // 2), jnp.bfloat16),
             pltpu.VMEM((slots, rows, chunk, width), jnp.bfloat16),
-            pltpu.VMEM((slots, halo_rows, width), jnp.bfloat16),
+            pltpu.VMEM((slots, halo_rows, width // 2), jnp.bfloat16),
             pltpu.VMEM((heads, members, lanes, keys), jnp.float32),
             pltpu.VMEM((groups, keys, 3 * lanes), jnp.bfloat16),
-            pltpu.VMEM((groups, lanes, lanes), jnp.bfloat16),
             pltpu.VMEM((members, ring, rows, chunk, width), jnp.bfloat16),
-            dma((2,)), dma((slots,)), dma((slots,)), dma((slots,)), dma((slots,)),
-            dma((slots,)), dma((slots,)), dma,
+            dma((5,)), dma((slots,)), dma((slots,)), dma((slots,)), dma((slots,)),
+            dma((slots,)), dma((slots,)),
         ],
         compiler_params=pltpu.CompilerParams(
-            collective_id=0, has_side_effects=True, vmem_limit_bytes=40 * 1024 * 1024
+            collective_id=0, has_side_effects=True, vmem_limit_bytes=62 * 1024 * 1024
         ),
-    )(tokens, w_qkv, w_out, rel_bias, gain.reshape(1, width))
+    )(tokens, w_qkv, w_out, jnp.transpose(rel_bias, (1, 2, 3, 0)), gain.reshape(1, width))
 
 
 def solution(mesh):

time: 33.3 us -> 26.1 us (0.78)
  local copies, waits for them, and re-layouts: 5.9 us -> 1.67 us
  Pallas kernels: 27.1 us -> 24.3 us
    unnamed x10 -> x1, local copies, waits for them, and re-layouts: 5.9 us -> 1.67 us
    pallas_call x1, Pallas kernels: 27.1 us -> 24.3 us  [fused(): pl.pallas_call(body_of, out_shape=jax.ShapeDtypeStruct(tokens.shape, jnp....]
where the time goes in v1:
time: 26.1 us; the launch traced here: 26 us
  Pallas kernels  24.3 us (93%)
  local copies, waits for them, and re-layouts  1.67 us (6%)
    pallas_call x1, Pallas kernels, fused(): pl.pallas_call(body_of, out_shape=jax.ShapeDtypeStruct(tokens.shape, jnp....  24.3 us
    unnamed x1, local copies, waits for them, and re-layouts  1.67 us

profile of v1, /device:TPU:0, one launch (start us, length us, event | category | flops | bytes accessed | tf_op | source)
XLA Modules:
  0.0 26.0 jit_solution(5233017745301908955)
XLA Ops:
  0.0 24.3 %shard_map.55 = bf16[1,2,2,64,512]{4,3,2,1,0:T(8,128)(2,1)} custom-call(bf16[1,2,2,64,512]{4,3,2,1,0:T(8,128)(2,1)} %tok_hbm.1, bf16[512,1536]{1,0:T(8,128)(2,1)} %wqkv_ref.1, bf16[512,512]{1,0:T(8,128)(2,1)} %wout_ref.1, f32[5,5,5,16]{3,2,1,0:T(8,128)} %bitcast.2, f32[1,512]{1,0:T(1,128)} %bitcast.3), custom_call_target="tpu_custom_call" | custom-call | tf_op jit(solution)/shard_map/pallas_call | solution.py:454
  24.3 1.7 %copy.7 = bf16[1,2,2,64,512]{4,3,2,1,0:T(8,128)(2,1)} copy(bf16[1,2,2,64,512]{4,3,2,1,0:T(8,128)(2,1)} %shard_map.55) | data formatting | bytes 524288

commit v2 on v1

--- a/solution.py
+++ b/solution.py
@@ -146,7 +146,7 @@
     members, ring, half, tap_groups, radius, scale,
     tok_hbm, wqkv_ref, wout_ref, bias_hbm, gain_hbm, out_ref,
     tok_ref, bias_ref, gain_ref, wqkv, wout, regrouped, halo_out, main_in, halo_in, bias_full, qkv, returned,
-    weight_sems, main_send, main_recv, halo_send, halo_recv, back_send, back_recv,
+    weight_sems, main_send, main_recv, halo_send, halo_recv, back_send, back_recv, local_sem,
 ):
     kernel, heads = bias_ref.shape[0], bias_ref.shape[3]
     rows, x_cells, width = tok_ref.shape[2:]
@@ -381,7 +381,7 @@
             if dm == 0:
                 @pl.when(place == gy)
                 def _():
-                    out_ref[0, mine, :, own_columns, :] = returned[dm, place]
+                    pltpu.make_async_copy(going, landing, local_sem).start()
 
                 @pl.when(place != gy)
                 def _():
@@ -413,6 +413,10 @@
             else:
                 pl.when(place != gy)(finish)
 
+                @pl.when(place == gy)
+                def _():
+                    pltpu.make_async_copy(returned.at[dm, place], landing, local_sem).wait()
+
 
 def pair_plan(mesh_shape, depth_total, shapes):
     boxes, planes, rows, x_cells, width, heads, kernel = shapes
@@ -444,7 +448,6 @@
     halo_rows = 2 * rows * halo_slots
     members, slots = planes, planes * ring
     keys = 3 * lanes
-    vmem = pl.BlockSpec(memory_space=pltpu.VMEM)
     hbm = pl.BlockSpec(memory_space=pltpu.HBM)
     body_of = functools.partial(
         kernel_body, members, ring, depth_devices // 2, tap_groups, kernel // 2,
@@ -455,7 +458,7 @@
         body_of,
         out_shape=jax.ShapeDtypeStruct(tokens.shape, jnp.bfloat16),
         in_specs=[hbm] * 5,
-        out_specs=vmem,
+        out_specs=hbm,
         scratch_shapes=[
             pltpu.VMEM(tokens.shape, jnp.bfloat16),
             pltpu.VMEM(rel_bias.shape[1:] + (heads,), jnp.float32),
@@ -470,7 +473,7 @@
             pltpu.VMEM((groups, keys, 3 * lanes), jnp.bfloat16),
             pltpu.VMEM((members, ring, rows, chunk, width), jnp.bfloat16),
             dma((5,)), dma((slots,)), dma((slots,)), dma((slots,)), dma((slots,)),
-            dma((slots,)), dma((slots,)),
+            dma((slots,)), dma((slots,)), dma,
         ],
         compiler_params=pltpu.CompilerParams(
             collective_id=0, has_side_effects=True, vmem_limit_bytes=62 * 1024 * 1024

time: 26.1 us -> 25.6 us (0.981)
  Pallas kernels: 24.3 us -> 23.8 us
    pallas_call x1, Pallas kernels: 24.3 us -> 23.8 us  [fused(): pl.pallas_call(body_of, out_shape=jax.ShapeDtypeStruct(tokens.shape, jnp....]
where the time goes in v2:
time: 25.6 us; the launch traced here: 25.4 us
  Pallas kernels  23.8 us (93%)
  local copies, waits for them, and re-layouts  1.67 us (7%)
    pallas_call x1, Pallas kernels, fused(): pl.pallas_call(body_of, out_shape=jax.ShapeDtypeStruct(tokens.shape, jnp....  23.8 us
    unnamed x1, local copies, waits for them, and re-layouts  1.67 us

profile of v2, /device:TPU:0, one launch (start us, length us, event | category | flops | bytes accessed | tf_op | source)
XLA Modules:
  0.0 25.4 jit_solution(16307639041189505615)
XLA Ops:
  0.0 23.8 %shard_map.55 = bf16[1,2,2,64,512]{4,3,2,1,0:T(8,128)(2,1)} custom-call(bf16[1,2,2,64,512]{4,3,2,1,0:T(8,128)(2,1)} %tok_hbm.1, bf16[512,1536]{1,0:T(8,128)(2,1)} %wqkv_ref.1, bf16[512,512]{1,0:T(8,128)(2,1)} %wout_ref.1, f32[5,5,5,16]{3,2,1,0:T(8,128)} %bitcast.2, f32[1,512]{1,0:T(1,128)} %bitcast.3), custom_call_target="tpu_custom_call" | custom-call | tf_op jit(solution)/shard_map/pallas_call | solution.py:457
  23.8 1.7 %copy.7 = bf16[1,2,2,64,512]{4,3,2,1,0:T(8,128)(2,1)} copy(bf16[1,2,2,64,512]{4,3,2,1,0:T(8,128)(2,1)} %shard_map.55) | data formatting | bytes 524288
